TPU v7x, 32 devices: a whole 2x2x4 slice. The times are simulated.
32 devices in a mesh: groups: 2 (over y), tensor: 16 (over z, x, core).
Axes of the slice: x: 2, y: 2, z: 4, core: 2. Of those that a mesh axis runs over, the one named last changes fastest.
Arguments:
- token_ids: int32 [16, 4], P('tensor', 'groups'), parts along dimension 1, may hold values from 0 to 63
- lengths: int32 [4], P('groups'), parts along dimension 0, may hold values from 8 to 16, as said below
- embed_table: bfloat16 [64, 6144], replicated, may hold values from -6 to 6
- gain_attn: float32 [6144], replicated, may hold values from 0.1 to 1.9
- w_qkv: bfloat16 [6144, 18432], P(None, 'tensor'), may hold values from -0.078125 to 0.078125
- w_out: bfloat16 [6144, 6144], P(None, 'tensor'), may hold values from -0.078125 to 0.078125
- gain_first: float32 [6144], replicated, may hold values from 0.1 to 1.9
- gate_first: bfloat16 [6144, 16384], P(None, 'tensor'), may hold values from -0.078125 to 0.078125
- up_first: bfloat16 [6144, 16384], P(None, 'tensor'), may hold values from -0.078125 to 0.078125
- down_first: bfloat16 [16384, 6144], P('tensor'), may hold values from -0.09375 to 0.09375
- gain_second: float32 [6144], replicated, may hold values from 0.1 to 1.9
- gate_second: bfloat16 [6144, 16384], P(None, 'tensor'), may hold values from -0.078125 to 0.078125
- up_second: bfloat16 [6144, 16384], P(None, 'tensor'), may hold values from -0.078125 to 0.078125
- down_second: bfloat16 [16384, 6144], P('tensor'), may hold values from -0.09375 to 0.09375
Outputs:
- states: bfloat16 [16, 4, 6144], P('tensor', 'groups'), parts along dimension 1
There are 2 independent parts, one for each index of `groups`. A program takes and returns all parts, laid end to end along the dimension named above; an argument that names none is the same for every part. Nothing has to cross between parts.
Inputs may be any that keep to these rules, and one draw needn't show every extreme that they name: `lengths`: each micro-batch holds one protein of at least half of 16 positions; in every draw one micro-batch is full, 16 positions.
All inputs are finite; a program needn't handle non-finite values.
Results may differ from a plain program's by a relative error of at most 0.013.
Values may be sent and summed in bfloat16 or wider, within the bound.
A program may use at most 192 MiB of HBM per device.

v0:
```python
import jax
import jax.numpy as jnp
from jax import lax
from jax.sharding import PartitionSpec as P

H = 48
HD = 128


def norm_rows(values, gain_vec):
    row_mean = jnp.mean(values, axis=-1, keepdims=True)
    centred = values - row_mean
    row_var = jnp.mean(centred * centred, axis=-1, keepdims=True)
    return (centred * lax.rsqrt(row_var + 1e-05) * gain_vec).astype(jnp.bfloat16)


def local_hidden(normed, gate_mat, up_mat):
    gated = jnp.einsum("pmd,dc->pmc", normed, gate_mat, preferred_element_type=jnp.float32)
    lifted = jnp.einsum("pmd,dc->pmc", normed, up_mat, preferred_element_type=jnp.float32)
    return (jax.nn.silu(gated) * lifted).astype(jnp.bfloat16)


def spread_rows(local_rows, row_fn):
    return row_fn(lax.all_gather(local_rows, "tensor", axis=0, tiled=True), jnp.int32(0))


def to_tokens(columns):
    return lax.all_to_all(columns, "tensor", split_axis=0, concat_axis=2, tiled=True)


def down_sum(hidden_all, down_mat):
    return lax.psum_scatter(
        jnp.einsum("pmc,cd->pmd", hidden_all, down_mat, preferred_element_type=jnp.float32),
        "tensor",
        scatter_dimension=0,
        tiled=True,
    )


def local(
    token_ids,
    lengths,
    embed_table,
    gain_attn,
    w_qkv,
    w_out,
    gain_first,
    gate_first,
    up_first,
    down_first,
    gain_second,
    gate_second,
    up_second,
    down_second,
):
    rows_here = token_ids.shape[0]
    micro_count = token_ids.shape[1]
    vocab_size = embed_table.shape[0]
    own_start = lax.axis_index("tensor") * rows_here
    onehot = (token_ids[:, :, None] == jnp.arange(vocab_size)[None, None, :]).astype(jnp.bfloat16)
    embedded = jnp.einsum("pmv,vd->pmd", onehot, embed_table, preferred_element_type=jnp.float32)
    normed_attn = norm_rows(embedded, gain_attn)

    def qkv_rows(row_piece, row_start):
        return jnp.einsum(
            "pmd,dc->pmc", row_piece, w_qkv, preferred_element_type=jnp.float32
        ).astype(jnp.bfloat16)

    projected = to_tokens(spread_rows(normed_attn, qkv_rows))
    feat_width = projected.shape[2] // 3
    queries = projected[..., :feat_width].reshape(rows_here, micro_count, H, HD)
    key_rows = projected[..., feat_width : 2 * feat_width]
    value_rows = projected[..., 2 * feat_width :]
    score_scale = HD ** (-0.5)
    key_piece = lax.all_gather(key_rows, "tensor", axis=0, tiled=True)
    value_piece = lax.all_gather(value_rows, "tensor", axis=0, tiled=True)
    piece_rows = key_piece.shape[0]
    key_heads = key_piece.reshape(piece_rows, micro_count, H, HD)
    value_heads = value_piece.reshape(piece_rows, micro_count, H, HD)
    scores = (
        jnp.einsum("pmhe,qmhe->pmhq", queries, key_heads, preferred_element_type=jnp.float32)
        * score_scale
    )
    positions = jnp.arange(piece_rows)
    live_keys = (positions[None, :] < lengths[:, None]).astype(jnp.float32)
    weights = jnp.exp(scores) * live_keys[None, :, None, :]
    denominator = jnp.sum(weights, axis=-1)
    numerator = jnp.einsum(
        "pmhq,qmhe->pmhe",
        weights.astype(jnp.bfloat16),
        value_heads,
        preferred_element_type=jnp.float32,
    )
    numerator, denominator = (numerator, denominator)
    attended = (
        (numerator / denominator[..., None])
        .reshape(rows_here, micro_count, feat_width)
        .astype(jnp.bfloat16)
    )

    def out_rows(row_piece, row_start):
        return jnp.einsum(
            "pmd,dc->pmc", row_piece, w_out, preferred_element_type=jnp.float32
        ).astype(jnp.bfloat16)

    after_attn = embedded + to_tokens(spread_rows(attended, out_rows)).astype(jnp.float32)

    def first_rows(row_piece, row_start):
        return local_hidden(row_piece, gate_first, up_first)

    hidden_first = spread_rows(norm_rows(after_attn, gain_first), first_rows)
    partial_all = jnp.einsum(
        "pmc,cd->pmd", hidden_first, down_first, preferred_element_type=jnp.float32
    )
    own_rows = lax.dynamic_slice_in_dim(partial_all, own_start, rows_here, 0) + after_attn
    partial_all = lax.dynamic_update_slice_in_dim(partial_all, own_rows, own_start, 0)
    first_all = lax.psum(partial_all, "tensor")
    after_first = lax.dynamic_slice_in_dim(first_all, own_start, rows_here, 0)
    hidden_second = local_hidden(norm_rows(first_all, gain_second), gate_second, up_second)
    after_second = after_first + down_sum(hidden_second, down_second)
    return after_second.astype(jnp.bfloat16)


def solution(mesh):
    return jax.shard_map(
        local,
        mesh=mesh,
        in_specs=(
            P("tensor", "groups"),
            P("groups"),
            P(),
            P(),
            P(None, "tensor"),
            P(None, "tensor"),
            P(),
            P(None, "tensor"),
            P(None, "tensor"),
            P("tensor", None),
            P(),
            P(None, "tensor"),
            P(None, "tensor"),
            P("tensor", None),
        ),
        out_specs=P("tensor", "groups", None),
        check_vma=False,
    )
```

profile of v0, /device:TPU:0, one launch (start us, length us, event | category | flops | bytes accessed | tf_op | source)
XLA Modules:
  0.0 382.2 jit_solution(4767694113768598177)
XLA Ops:
  6.5 0.0 copy-start
  6.5 0.0 copy-start.5
  6.5 1.1 copy-done
  7.7 1.0 fusion.79
  8.7 0.2 multiply_reduce_fusion.2
  9.0 0.8 fusion.64
  9.8 24.1 %all-gather.2 = bf16[16,2,6144]{2,1,0:T(2,128)(2,1)S(1)} all-gather(bf16[1,2,6144]{2,1,0:T(2,128)(2,1)S(1)} %fusion.64), channel_id=2, replica_groups=mesh['groups'=2,'tensor'=16] {'tensor'}, dimensions={0}, use_global_device_ids=true | all-gather | bytes 417792 | tf_op jit(solution)/shard_map/all_gather | solution.py:24
  34.0 0.0 copy-start.3
  34.0 7.6 %fusion.16 = bf16[16,2,1152]{2,0,1:T(8,128)(2,1)S(1)} fusion(bf16[6144,1152]{1,0:T(8,128)(2,1)} %param.18, bf16[16,2,6144]{2,1,0:T(2,128)(2,1)S(1)} %all-gather.2), kind=kOutput, calls=%fused_computation.16 | convolution fusion | flops 453021696 | bytes 14622720 | tf_op jit(solution)/shard_map/pmd,dc->pmc/dot_general | solution.py:65
  41.5 0.7 copy.49
  42.2 3.5 all-to-all-start
  45.7 0.0 copy-done.5
  45.7 0.1 compare_convert_fusion
  45.8 6.9 %all-to-all-done = bf16[16,2,1152]{2,1,0:T(2,128)(2,1)S(1)} async-done(((bf16[16,2,1152]{2,1,0:T(2,128)(2,1)}), bf16[16,2,1152]{2,1,0:T(2,128)(2,1)S(1)}, u32[]{:S(2)}, u32[]{:S(2)}) %all-to-all-start) | async-done | bytes 73760 | tf_op jit(solution)/shard_map/all_to_all | solution.py:28
  52.7 0.1 fusion.78
  52.8 18.8 %all_gather.17 = bf16[16,2,6144]{2,1,0:T(2,128)(2,1)S(1)} all-gather(bf16[1,2,6144]{2,1,0:T(2,128)(2,1)S(1)} %get-tuple-element.9), channel_id=1, replica_groups=mesh['groups'=2,'tensor'=16] {'tensor'}, dimensions={0}, use_global_device_ids=true | all-gather | bytes 417792 | tf_op jit(solution)/shard_map/all_gather | solution.py:75
  71.6 0.2 reshape.163
  71.9 0.3 fusion.40
  72.2 0.1 copy.61
  72.3 0.1 fusion.68
  72.4 0.1 copy.63
  72.5 19.6 %all_gather.16 = bf16[16,2,6144]{2,1,0:T(2,128)(2,1)S(1)} all-gather(bf16[1,2,6144]{2,1,0:T(2,128)(2,1)S(1)} %get-tuple-element.7), channel_id=1, replica_groups=mesh['groups'=2,'tensor'=16] {'tensor'}, dimensions={0}, use_global_device_ids=true | all-gather | bytes 417792 | tf_op jit(solution)/shard_map/all_gather | solution.py:76
  92.0 0.2 reshape.162
  92.3 0.2 fusion.38
  92.5 0.1 divide_convert_fusion
  92.7 19.0 %all_gather.18 = bf16[16,2,6144]{2,1,0:T(2,128)(2,1)S(1)} all-gather(bf16[1,2,6144]{2,1,0:T(2,128)(2,1)S(1)} %convert_element_type.75), channel_id=1, replica_groups=mesh['groups'=2,'tensor'=16] {'tensor'}, dimensions={0}, use_global_device_ids=true | all-gather | bytes 417792 | tf_op jit(solution)/shard_map/all_gather | solution.py:24
  111.7 3.1 fusion.35
  114.8 0.6 copy.51
  115.5 3.5 all-to-all-start.1
  119.0 0.0 all-reduce.4.cloned.1.call-start
  119.0 6.5 %all-to-all-done.1 = bf16[16,2,384]{2,1,0:T(2,128)(2,1)S(1)} async-done(((bf16[16,2,384]{2,1,0:T(2,128)(2,1)}), bf16[16,2,384]{2,1,0:T(2,128)(2,1)S(1)}, u32[]{:S(2)}, u32[]{:S(2)}) %all-to-all-start.1) | async-done | bytes 24608 | tf_op jit(solution)/shard_map/all_to_all | solution.py:28
  125.5 0.2 fusion.77
  125.7 0.2 multiply_reduce_fusion.1
  125.9 0.0 copy-done.3
  126.0 0.1 fusion.65
  126.1 18.6 %all-gather.3 = bf16[16,2,6144]{2,1,0:T(2,128)(2,1)S(1)} all-gather(bf16[1,2,6144]{2,1,0:T(2,128)(2,1)S(1)} %fusion.65), channel_id=3, replica_groups=mesh['groups'=2,'tensor'=16] {'tensor'}, dimensions={0}, use_global_device_ids=true | all-gather | bytes 417792 | tf_op jit(solution)/shard_map/all_gather | solution.py:24
  144.7 6.8 %fusion.12 = f32[16,2,1024]{2,0,1:T(8,128)S(1)} fusion(bf16[6144,1024]{1,0:T(8,128)(2,1)} %param.21, bf16[16,2,6144]{2,1,0:T(2,128)(2,1)S(1)} %all-gather.3), kind=kOutput, calls=%fused_computation.12 | convolution fusion | flops 402653184 | bytes 13107200 | tf_op jit(solution)/shard_map/pmd,dc->pmc/dot_general | solution.py:18
  151.5 0.0 copy-start.4
  151.5 12.6 %fusion.8 = f32[16,2,6144]{2,0,1:T(8,128)S(1)} fusion(bf16[1024,6144]{1,0:T(8,128)(2,1)} %param.23, bf16[6144,1024]{1,0:T(8,128)(2,1)} %param.22, bf16[16,2,6144]{2,1,0:T(2,128)(2,1)S(1)} %all-gather.3, f32[16,2,1024]{2,0,1:T(8,128)S(1)} %fusion.12), kind=kOutput, calls=%fused_computation.8 | convolution fusion | flops 805502976 | bytes 26476544 | tf_op jit(solution)/shard_map/pmc,cd->pmd/dot_general | solution.py:112
  164.2 0.6 copy.55
  164.8 0.0 copy-start.2
  164.8 0.9 copy-done.2
  165.7 0.0 all-reduce.4.cloned.1.call-update
  165.8 0.2 all-reduce.6.cloned.1.call-start
  166.0 90.3 %all-reduce.4.cloned.1.call-done = f32[16,2,6144]{2,1,0:T(2,128)} async-done(((f32[16,2,6144]{2,1,0:T(2,128)}), f32[16,2,6144]{2,1,0:T(2,128)}) %all-reduce.4.cloned.1.call-update) | async-done | bytes 786448 | tf_op jit(solution)/shard_map/psum | solution.py:117
  256.3 1.4 reduce_sum.68
  257.7 1.7 multiply_reduce_fusion
  259.4 0.0 copy-done.4
  259.4 1.7 multiply_convert_fusion
  261.1 0.0 copy-start.1
  261.1 6.9 %fusion.6 = f32[16,2,1024]{2,0,1:T(8,128)S(1)} fusion(bf16[6144,1024]{1,0:T(8,128)(2,1)} %param.25, bf16[16,2,6144]{2,1,0:T(2,128)(2,1)S(1)} %multiply_convert_fusion), kind=kOutput, calls=%fused_computation.6 | convolution fusion | flops 402653184 | bytes 13107200 | tf_op jit(solution)/shard_map/pmd,dc->pmc/dot_general | solution.py:18
  268.0 0.0 copy-start.6
  268.0 12.6 %fusion.2 = f32[16,2,6144]{2,0,1:T(8,128)S(1)} fusion(bf16[1024,6144]{1,0:T(8,128)(2,1)} %param.27, bf16[6144,1024]{1,0:T(8,128)(2,1)} %param.26, bf16[16,2,6144]{2,1,0:T(2,128)(2,1)S(1)} %multiply_convert_fusion, f32[16,2,1024]{2,0,1:T(8,128)S(1)} %fusion.6), kind=kOutput, calls=%fused_computation.2 | convolution fusion | flops 805502976 | bytes 26476544 | tf_op jit(solution)/shard_map/pmc,cd->pmd/dot_general | solution.py:33
  280.6 1.5 copy.58
  282.2 0.0 all-reduce.6.cloned.1.call-update
  282.2 0.0 copy-done.6
  282.2 0.6 dynamic-slice
  282.8 90.5 %all-reduce.6.cloned.1.call-done = f32[16,2,6144]{2,1,0:T(2,128)} async-done(((f32[16,2,6144]{2,1,0:T(2,128)}), f32[16,2,6144]{2,1,0:T(2,128)}) %all-reduce.6.cloned.1.call-update) | async-done | bytes 786448
  373.3 2.0 fusion.62
  375.3 0.0 copy-done.1
  (10 shorter events, 0.1 us)
Async XLA Ops:
  6.5 1.1 copy-start
  6.5 39.2 %copy-start.5 = (s32[2]{0:T(128)S(1)}, s32[2]{0:T(128)}, u32[]{:S(2)}) copy-start(s32[2]{0:T(128)} %param.15) | copy-start | bytes 28
  34.0 92.0 %copy-start.3 = (f32[6144]{0:T(1024)S(1)}, f32[6144]{0:T(1024)}, u32[]{:S(2)}) copy-start(f32[6144]{0:T(1024)} %param.20) | copy-start | bytes 73732
  42.2 10.5 %all-to-all-start = ((bf16[16,2,1152]{2,1,0:T(2,128)(2,1)}), bf16[16,2,1152]{2,1,0:T(2,128)(2,1)S(1)}, u32[]{:S(2)}, u32[]{:S(2)}) async-start(bf16[16,2,1152]{2,1,0:T(2,128)(2,1)} %copy.49), calls=%async_computation | async-start | bytes 147456 | tf_op jit(solution)/shard_map/all_to_all | solution.py:28
  115.5 10.0 %all-to-all-start.1 = ((bf16[16,2,384]{2,1,0:T(2,128)(2,1)}), bf16[16,2,384]{2,1,0:T(2,128)(2,1)S(1)}, u32[]{:S(2)}, u32[]{:S(2)}) async-start(bf16[16,2,384]{2,1,0:T(2,128)(2,1)} %copy.51), calls=%async_computation.1 | async-start | bytes 49152 | tf_op jit(solution)/shard_map/all_to_all | solution.py:28
  119.0 137.3 %all-reduce.4.cloned.1.call-start = ((), (), s32[]{:S(2)}) async-start(), calls=%async_computation.2 | async-start | bytes 1572864 | tf_op jit(solution)/shard_map/psum | solution.py:117
  151.5 107.9 %copy-start.4 = (f32[6144]{0:T(1024)S(1)}, f32[6144]{0:T(1024)}, u32[]{:S(2)}) copy-start(f32[6144]{0:T(1024)} %param.24) | copy-start | bytes 73732
  164.8 0.9 copy-start.2
  165.8 207.6 %all-reduce.6.cloned.1.call-start = ((), (), s32[]{:S(2)}) async-start(), calls=%async_computation.3 | async-start | bytes 1572864
  261.1 114.2 %copy-start.1 = (bf16[64,6144]{1,0:T(8,128)(2,1)S(1)}, bf16[64,6144]{1,0:T(8,128)(2,1)}, u32[]{:S(2)}) copy-start(bf16[64,6144]{1,0:T(8,128)(2,1)} %param.16) | copy-start | bytes 2359300
  268.0 14.2 %copy-start.6 = (u32[32]{0:T(128)S(1)}, u32[32]{0:T(128)}, u32[]{:S(2)}) copy-start(u32[32]{0:T(128)} %constant.31) | copy-start | bytes 388
Sparse Core Ops, SparseCore 0:
  165.9 90.3 all-reduce.3
  282.3 90.9 all-reduce.5
where the time goes:
time: 383 us; the launch traced here: 382 us
  waiting for transfers between devices  194 us (51%)
  blocking collectives  100 us (26%)
  matrix products  51.3 us (13%)
  between operations  13.6 us (4%)
  other arithmetic  8.77 us (2%)
  starting transfers between devices  7.26 us (2%)
  local copies, waits for them, and re-layouts  6.84 us (2%)
    unnamed x3, waiting for transfers between devices  90.6 us
    psum x1, waiting for transfers between devices, local(): first_all = lax.psum(partial_all, 'tensor')  90.3 us
    all_gather x3, blocking collectives, spread_rows(): lax.all_gather(local_rows, 'tensor', axis=0, tiled=True)  61.8 us
    all_gather x1, blocking collectives, local(): value_piece = lax.all_gather(value_rows, 'tensor', axis=0, tiled=True)  19.6 us
    all_gather x1, blocking collectives, local(): key_piece = lax.all_gather(key_rows, 'tensor', axis=0, tiled=True)  18.8 us
    dot_general x2, matrix products, local_hidden(): jnp.einsum('pmd,dc->pmc', normed, gate_mat, preferred_element_type=jnp.fl...  13.7 us
    all_to_all x2, waiting for transfers between devices, to_tokens(): lax.all_to_all(columns, 'tensor', split_axis=0, concat_axis=2, tiled=True)  13.4 us
    dot_general x1, matrix products, down_sum(): jnp.einsum('pmc,cd->pmd', hidden_all, down_mat, preferred_element_type=jn...  12.6 us
  transfers between devices with their start and end apart: 4, of which 4 were waited for; matrix products, arithmetic and copies ran while one was open for 0% of the time, Pallas kernels for 0%

commit v1 on v0

v1 whole, which is shorter than its diff:
```python
import functools

import jax
import jax.numpy as jnp
from jax import lax
from jax.experimental import pallas as pl
from jax.experimental.pallas import tpu as pltpu
from jax.sharding import PartitionSpec as P

HD = 128
LANES = 128
MESH = pl.DeviceIdType.MESH
F32 = jnp.float32
BF16 = jnp.bfloat16


def norm_rows(values, gain_vec):
    row_mean = jnp.mean(values, axis=-1, keepdims=True)
    centred = values - row_mean
    row_var = jnp.mean(centred * centred, axis=-1, keepdims=True)
    return (centred * lax.rsqrt(row_var + 1e-05) * gain_vec).astype(jnp.bfloat16)


def local_hidden(normed, gate_mat, up_mat):
    gated = jnp.einsum("pmd,dc->pmc", normed, gate_mat, preferred_element_type=jnp.float32)
    lifted = jnp.einsum("pmd,dc->pmc", normed, up_mat, preferred_element_type=jnp.float32)
    return (jax.nn.silu(gated) * lifted).astype(jnp.bfloat16)


def spread_rows(local_rows, row_fn):
    return row_fn(lax.all_gather(local_rows, "tensor", axis=0, tiled=True))


def to_tokens(columns):
    return lax.all_to_all(columns, "tensor", split_axis=0, concat_axis=2, tiled=True)


def local_general(
    token_ids, lengths, embed_table, gain_attn, w_qkv, w_out,
    gain_first, gate_first, up_first, down_first,
    gain_second, gate_second, up_second, down_second,
):
    rows_here, micro_count = token_ids.shape
    vocab_size, width = embed_table.shape
    heads = width // HD
    own_start = lax.axis_index("tensor") * rows_here
    onehot = (token_ids[:, :, None] == jnp.arange(vocab_size)[None, None, :]).astype(jnp.bfloat16)
    embedded = jnp.einsum("pmv,vd->pmd", onehot, embed_table, preferred_element_type=jnp.float32)

    def matmul_rows(weight):
        return lambda rows: jnp.einsum(
            "pmd,dc->pmc", rows, weight, preferred_element_type=jnp.float32
        ).astype(jnp.bfloat16)

    projected = to_tokens(spread_rows(norm_rows(embedded, gain_attn), matmul_rows(w_qkv)))
    queries = projected[..., :width].reshape(rows_here, micro_count, heads, HD)
    keys = lax.all_gather(projected[..., width : 2 * width], "tensor", axis=0, tiled=True)
    values = lax.all_gather(projected[..., 2 * width :], "tensor", axis=0, tiled=True)
    total = keys.shape[0]
    keys = keys.reshape(total, micro_count, heads, HD)
    values = values.reshape(total, micro_count, heads, HD)
    scores = jnp.einsum("pmhe,qmhe->pmhq", queries, keys, preferred_element_type=jnp.float32)
    live = (jnp.arange(total)[None, :] < lengths[:, None]).astype(jnp.float32)
    weights = jnp.exp(scores * HD ** (-0.5)) * live[None, :, None, :]
    numerator = jnp.einsum(
        "pmhq,qmhe->pmhe", weights.astype(jnp.bfloat16), values, preferred_element_type=jnp.float32
    )
    attended = numerator / jnp.sum(weights, axis=-1)[..., None]
    attended = attended.reshape(rows_here, micro_count, width).astype(jnp.bfloat16)
    after_attn = embedded + to_tokens(spread_rows(attended, matmul_rows(w_out))).astype(jnp.float32)
    hidden_first = spread_rows(
        norm_rows(after_attn, gain_first), lambda rows: local_hidden(rows, gate_first, up_first)
    )
    partial_all = jnp.einsum(
        "pmc,cd->pmd", hidden_first, down_first, preferred_element_type=jnp.float32
    )
    own_rows = lax.dynamic_slice_in_dim(partial_all, own_start, rows_here, 0) + after_attn
    partial_all = lax.dynamic_update_slice_in_dim(partial_all, own_rows, own_start, 0)
    first_all = lax.psum(partial_all, "tensor")
    after_first = lax.dynamic_slice_in_dim(first_all, own_start, rows_here, 0)
    hidden_second = local_hidden(norm_rows(first_all, gain_second), gate_second, up_second)
    second = jnp.einsum(
        "pmc,cd->pmd", hidden_second, down_second, preferred_element_type=jnp.float32
    )
    after_second = after_first + lax.psum_scatter(
        second, "tensor", scatter_dimension=0, tiled=True
    )
    return after_second.astype(jnp.bfloat16)


def fused_kernel(
    n, micro, vocab, kc,
    tok_ref, len_ref, emb_hbm, ga_hbm, wq_hbm, wo_hbm,
    gf_hbm, g1_hbm, u1_hbm, d1_hbm, gs_hbm, g2_hbm, u2_hbm, d2_hbm,
    out_ref,
    buf_a, buf_o, buf_g, buf_u, buf_d,
    emb_ref, gain_ref,
    toks, onehot, resid, normed, blocks, qkv, full, acc, cout, crecv, xout, xrecv, zout, zrecv,
    own, fin, finr, rows_out,
    w_sem, e_sem, small_send, small_recv, q_send, q_recv, ag_send, ag_recv,
    rs_send, rs_recv, f_send, f_recv,
):
    width = emb_ref.shape[1]
    pos = n
    rows = micro * pos
    shard = width // n
    hidden_cols = buf_g.shape[1]
    hpd = width // HD // n
    nblk = 3 * hpd
    heads = width // HD
    nz = n // 4
    chunks = width // kc
    sub = shard // LANES

    me = lax.axis_index("tensor")
    grp = lax.axis_index("groups")
    core = lax.rem(me, 2)
    xbit = lax.rem(me // 2, 2)
    zpos = me // 4
    cpeer = me + 1 - 2 * core
    xpeer = me + 2 - 4 * xbit

    def zmove(dev, k):
        return lax.rem(dev + 4 * k + n, n)

    def rcopy(src, dst, ssem, rsem, dev):
        return pltpu.make_async_remote_copy(
            src_ref=src, dst_ref=dst, send_sem=ssem, recv_sem=rsem,
            device_id=(grp, dev), device_id_type=MESH,
        )

    def row_chunk(ref, c):
        return ref.at[pl.ds(c * kc, kc)]

    dk = hidden_cols // 4

    def w_copies(which):
        if which == "q":
            return [pltpu.make_async_copy(row_chunk(wq_hbm, c), row_chunk(buf_a, c), w_sem.at[0, c]) for c in range(chunks)]
        if which == "o":
            return [pltpu.make_async_copy(row_chunk(wo_hbm, c), row_chunk(buf_o, c), w_sem.at[1, c]) for c in range(chunks)]
        if which == "g1":
            return [pltpu.make_async_copy(row_chunk(g1_hbm, c), row_chunk(buf_g, c), w_sem.at[2, c]) for c in range(chunks)]
        if which == "u1":
            return [pltpu.make_async_copy(row_chunk(u1_hbm, c), row_chunk(buf_u, c), w_sem.at[3, c]) for c in range(chunks)]
        if which == "g2":
            return [
                pltpu.make_async_copy(
                    row_chunk(g2_hbm, c), buf_a.at[pl.ds(c * kc, kc), pl.ds(0, hidden_cols)], w_sem.at[4, c]
                )
                for c in range(chunks)
            ]
        if which == "u2":
            return [pltpu.make_async_copy(row_chunk(u2_hbm, c), row_chunk(buf_g, c), w_sem.at[5, c]) for c in range(chunks)]
        src = d1_hbm if which == "d1" else d2_hbm
        row = 6 if which == "d1" else 7
        return [
            pltpu.make_async_copy(src.at[pl.ds(c * dk, dk)], buf_d.at[pl.ds(c * dk, dk)], w_sem.at[row, c])
            for c in range(4)
        ]

    def start_all(which):
        for cp in w_copies(which):
            cp.start()

    def wait_all(which):
        for cp in w_copies(which):
            cp.wait()

    small = [
        pltpu.make_async_copy(emb_hbm, emb_ref, e_sem.at[0]),
        pltpu.make_async_copy(ga_hbm, gain_ref.at[0], e_sem.at[1]),
        pltpu.make_async_copy(gf_hbm, gain_ref.at[1], e_sem.at[2]),
        pltpu.make_async_copy(gs_hbm, gain_ref.at[2], e_sem.at[3]),
    ]
    for cp in small:
        cp.start()
    start_all("q")
    start_all("o")
    start_all("g1")

    tile_row = lax.broadcasted_iota(jnp.int32, (8, LANES), 0)
    tile = jnp.zeros((8, LANES), jnp.int32)
    for m in range(micro):
        tile = jnp.where(tile_row == m, tok_ref[0, m], tile)
    toks[me] = tile

    barrier = pltpu.get_barrier_semaphore()
    for k in range(1, n):
        pl.semaphore_signal(barrier, inc=1, device_id=(grp, lax.rem(me + k, n)), device_id_type=MESH)
    pl.semaphore_wait(barrier, n - 1)

    tok_sends = [
        rcopy(toks.at[me], toks.at[me], small_send.at[k], small_recv.at[k], lax.rem(me + k, n))
        for k in range(1, n)
    ]
    for cp in tok_sends:
        cp.start()
    for k in range(1, n):
        src = lax.rem(me + n - k, n)
        rcopy(toks.at[src], toks.at[src], small_send.at[k], small_recv.at[k], src).wait_recv()

    lane = lax.broadcasted_iota(jnp.int32, (1, vocab), 1)
    for p in range(pos):
        for m in range(micro):
            onehot[m * pos + p : m * pos + p + 1, :] = (toks[p, m : m + 1, :vocab] == lane).astype(F32)
    for cp in small:
        cp.wait()
    hot = onehot[...].astype(BF16)
    for c in range(chunks):
        sl = slice(c * kc, (c + 1) * kc)
        resid[:, sl] = jnp.dot(hot, emb_ref[:, sl], preferred_element_type=F32)

    def norm_into(index):
        total = jnp.zeros((rows, 1), F32)
        for c in range(chunks):
            total += jnp.sum(resid[:, c * kc : (c + 1) * kc], axis=1, keepdims=True)
        mean = total * (1.0 / width)
        var = jnp.zeros((rows, 1), F32)
        for c in range(chunks):
            cen = resid[:, c * kc : (c + 1) * kc] - mean
            var += jnp.sum(cen * cen, axis=1, keepdims=True)
        inv = lax.rsqrt(var * (1.0 / width) + 1e-05)
        for c in range(chunks):
            sl = slice(c * kc, (c + 1) * kc)
            normed[:, sl] = ((resid[:, sl] - mean) * inv * gain_ref[index, :, sl]).astype(BF16)

    norm_into(0)

    part = jnp.zeros((rows, nblk * HD), F32)
    q_copies = w_copies("q")
    for c in range(chunks):
        q_copies[c].wait()
        part += jnp.dot(
            normed[:, c * kc : (c + 1) * kc], buf_a[c * kc : (c + 1) * kc, :], preferred_element_type=F32
        )
    for j in range(nblk):
        blocks[j] = part[:, j * HD : (j + 1) * HD].astype(BF16)

    def block_target(j):
        g = me * nblk + j
        kind = g // heads
        head = lax.rem(g, heads)
        return head // hpd, kind * hpd + lax.rem(head, hpd)

    for j in range(nblk):
        owner, slot = block_target(j)

        @pl.when(owner != me)
        def _():
            rcopy(blocks.at[j], qkv.at[slot], q_send.at[j], q_recv.at[slot], owner).start()

        @pl.when(owner == me)
        def _():
            pltpu.make_async_copy(blocks.at[j], qkv.at[slot], q_recv.at[slot]).start()

    start_all("u1")
    start_all("d1")
    start_all("g2")

    for slot in range(nblk):
        pltpu.make_async_copy(blocks.at[0], qkv.at[slot], q_recv.at[slot]).wait()

    ri = lax.broadcasted_iota(jnp.int32, (rows, rows), 0)
    ci = lax.broadcasted_iota(jnp.int32, (rows, rows), 1)
    live = jnp.zeros((rows, rows), F32)
    for m in range(micro):
        inside = (ri >= m * pos) & (ri < (m + 1) * pos) & (ci >= m * pos) & (ci < m * pos + len_ref[m])
        live = jnp.where(inside, 1.0, live)
    for h in range(hpd):
        scores = lax.dot_general(
            qkv[h], qkv[hpd + h], (((1,), (1,)), ((), ())), preferred_element_type=F32
        ) * (HD ** (-0.5))
        weights = jnp.where(live > 0.5, jnp.exp(scores), 0.0)
        denominator = jnp.sum(weights, axis=1, keepdims=True)
        numerator = jnp.dot(weights.astype(BF16), qkv[2 * hpd + h], preferred_element_type=F32)
        full[0, me, :, h * HD : (h + 1) * HD] = (numerator / denominator).astype(BF16)

    def gather(ph):
        buf = full.at[ph]
        sends = []

        def send(slot, idx, dev):
            cp = rcopy(buf.at[slot], buf.at[slot], ag_send.at[ph, idx], ag_recv.at[ph, idx], dev)
            cp.start()
            sends.append(cp)

        def arrive(slot, idx):
            rcopy(buf.at[slot], buf.at[slot], ag_send.at[ph, idx], ag_recv.at[ph, idx], cpeer).wait_recv()

        xbase, cbase = nz, 2 * nz
        for k in range(1, nz):
            send(me, k, zmove(me, k))
        send(me, xbase, xpeer)
        send(me, cbase, cpeer)
        for k in range(1, nz):
            src = zmove(me, -k)
            arrive(src, k)
            send(src, xbase + k, xpeer)
            send(src, cbase + k, cpeer)
        for k in range(nz):
            src = zmove(xpeer, -k)
            arrive(src, xbase + k)
            send(src, cbase + nz + k, cpeer)
        xc = cpeer + 2 - 4 * xbit
        for k in range(nz):
            arrive(zmove(cpeer, -k), cbase + k)
            arrive(zmove(xc, -k), cbase + nz + k)
        return sends

    sends0 = gather(0)
    for s in range(n):
        normed[:, s * shard : (s + 1) * shard] = full[0, s]

    part = jnp.zeros((rows, shard), F32)
    o_copies = w_copies("o")
    for c in range(chunks):
        o_copies[c].wait()
        part += jnp.dot(
            normed[:, c * kc : (c + 1) * kc], buf_o[c * kc : (c + 1) * kc, :], preferred_element_type=F32
        )
    full[1, me] = part.astype(BF16)
    sends1 = gather(1)
    for s in range(n):
        sl = slice(s * shard, (s + 1) * shard)
        resid[:, sl] = resid[:, sl] + full[1, s].astype(F32)

    def feed(gate_buf, up_buf, names, index):
        norm_into(index)
        g_copies, u_copies = w_copies(names[0]), w_copies(names[1])
        gated = jnp.zeros((rows, hidden_cols), F32)
        lifted = jnp.zeros((rows, hidden_cols), F32)
        for c in range(chunks):
            x = normed[:, c * kc : (c + 1) * kc]
            g_copies[c].wait()
            gated += jnp.dot(x, gate_buf[c * kc : (c + 1) * kc, :hidden_cols], preferred_element_type=F32)
        for c in range(chunks):
            x = normed[:, c * kc : (c + 1) * kc]
            u_copies[c].wait()
            lifted += jnp.dot(x, up_buf[c * kc : (c + 1) * kc, :], preferred_element_type=F32)
        return (gated / (1.0 + jnp.exp(-gated)) * lifted).astype(BF16)

    def down_reduce(hidden, ph):
        sends = []
        for j in range(2 * nz):
            k = j % nz
            xsel = (1 - xbit) if j < nz else xbit
            q = lax.rem(zpos + k, nz) * 2 + xsel
            both = jnp.dot(
                hidden,
                buf_d[:, pl.ds(pl.multiple_of(q * 2 * shard, LANES), 2 * shard)],
                preferred_element_type=F32,
            )
            left, right = both[:, :shard], both[:, shard:]
            is_left = jnp.zeros((rows, shard), jnp.int32) + core == 0
            acc[j] = jnp.where(is_left, left, right)
            cout[ph, j] = jnp.where(is_left, right, left).astype(BF16)
            cp = rcopy(cout.at[ph, j], crecv.at[ph, j], rs_send.at[ph, j], rs_recv.at[ph, j], cpeer)
            cp.start()
            sends.append(cp)
        for k in range(nz):
            sends[k].wait_recv()
            xout[ph, k] = (acc[k] + crecv[ph, k].astype(F32)).astype(BF16)
            cp = rcopy(
                xout.at[ph, k], xrecv.at[ph, k],
                rs_send.at[ph, 2 * nz + k], rs_recv.at[ph, 2 * nz + k], xpeer,
            )
            cp.start()
            sends.append(cp)
        for k in list(range(1, nz)) + [0]:
            sends[nz + k].wait_recv()
            sends[2 * nz + k].wait_recv()
            val = acc[nz + k] + crecv[ph, nz + k].astype(F32) + xrecv[ph, k].astype(F32)
            if k:
                zout[ph, k] = val.astype(BF16)
                cp = rcopy(
                    zout.at[ph, k], zrecv.at[ph, k],
                    rs_send.at[ph, 3 * nz + k], rs_recv.at[ph, 3 * nz + k], zmove(me, k),
                )
                cp.start()
                sends.append(cp)
            else:
                own[...] = val
        for k in range(1, nz):
            sends[3 * nz + k - 1].wait_recv()
            own[...] = own[...] + zrecv[ph, k].astype(F32)
        return sends

    hidden = feed(buf_g, buf_u, ("g1", "u1"), 1)
    start_all("u2")
    wait_all("d1")
    sends2 = down_reduce(hidden, 0)
    start_all("d2")
    full[2, me] = own[...].astype(BF16)
    sends3 = gather(2)
    for s in range(n):
        sl = slice(s * shard, (s + 1) * shard)
        resid[:, sl] = resid[:, sl] + full[2, s].astype(F32)

    hidden = feed(buf_a, buf_g, ("g2", "u2"), 2)
    wait_all("d2")
    sends4 = down_reduce(hidden, 1)
    own[...] = own[...] + resid[:, pl.ds(pl.multiple_of(me * shard, LANES), shard)]

    for p in range(pos):
        for m in range(micro):
            for k in range(sub):
                fin[p, m * sub + k : m * sub + k + 1, :] = own[m * pos + p : m * pos + p + 1, k * LANES : (k + 1) * LANES]
    fin_sends = []
    for k in range(1, n):
        dev = lax.rem(me + k, n)
        cp = rcopy(fin.at[dev], finr.at[me], f_send.at[k], f_recv.at[k], dev)
        cp.start()
        fin_sends.append(cp)
    finr[me] = fin[me]
    for k in range(1, n):
        src = lax.rem(me + n - k, n)
        rcopy(fin.at[src], finr.at[src], f_send.at[k], f_recv.at[k], src).wait_recv()
    for s in range(n):
        for m in range(micro):
            for k in range(sub):
                lo = s * shard + k * LANES
                rows_out[m : m + 1, lo : lo + LANES] = finr[s, m * sub + k : m * sub + k + 1, :]
    out_ref[0] = rows_out[...].astype(BF16)

    for cp in tok_sends + sends0 + sends1 + sends2 + sends3 + sends4 + fin_sends:
        cp.wait_send()
    for j in range(nblk):
        owner, slot = block_target(j)

        @pl.when(owner != me)
        def _():
            rcopy(blocks.at[j], qkv.at[slot], q_send.at[j], q_recv.at[slot], owner).wait_send()


def local_fused(n, kc, *args):
    token_ids, lengths, embed_table = args[:3]
    micro = token_ids.shape[1]
    vocab, width = embed_table.shape
    rows = n * micro
    shard = width // n
    hidden_cols = args[7].shape[1]
    nblk = 3 * width // HD // n
    nz = n // 4
    chunks = width // kc
    tall = lambda gain: gain.reshape(1, width)
    operands = list(args)
    for at in (3, 6, 10):
        operands[at] = tall(args[at])
    smem = pl.BlockSpec(memory_space=pltpu.SMEM)
    hbm = pl.BlockSpec(memory_space=pl.ANY)
    dma = pltpu.SemaphoreType.DMA
    weight_bytes = sum(a.size * a.dtype.itemsize for a in args)
    return pl.pallas_call(
        functools.partial(fused_kernel, n, micro, vocab, kc),
        out_shape=jax.ShapeDtypeStruct((1, micro, width), BF16),
        in_specs=[smem, smem] + [hbm] * 12,
        out_specs=pl.BlockSpec(memory_space=pltpu.VMEM),
        scratch_shapes=[
            pltpu.VMEM((width, nblk * HD), BF16),
            pltpu.VMEM((width, shard), BF16),
            pltpu.VMEM((width, hidden_cols), BF16),
            pltpu.VMEM((width, hidden_cols), BF16),
            pltpu.VMEM((hidden_cols, width), BF16),
            pltpu.VMEM((vocab, width), BF16),
            pltpu.VMEM((3, 1, width), F32),
            pltpu.VMEM((n, 8, LANES), jnp.int32),
            pltpu.VMEM((rows, vocab), F32),
            pltpu.VMEM((rows, width), F32),
            pltpu.VMEM((rows, width), BF16),
            pltpu.VMEM((nblk, rows, HD), BF16),
            pltpu.VMEM((nblk, rows, HD), BF16),
            pltpu.VMEM((3, n, rows, shard), BF16),
            pltpu.VMEM((2 * nz, rows, shard), F32),
            pltpu.VMEM((2, 2 * nz, rows, shard), BF16),
            pltpu.VMEM((2, 2 * nz, rows, shard), BF16),
            pltpu.VMEM((2, nz, rows, shard), BF16),
            pltpu.VMEM((2, nz, rows, shard), BF16),
            pltpu.VMEM((2, nz, rows, shard), BF16),
            pltpu.VMEM((2, nz, rows, shard), BF16),
            pltpu.VMEM((rows, shard), F32),
            pltpu.VMEM((n, 8, LANES), F32),
            pltpu.VMEM((n, 8, LANES), F32),
            pltpu.VMEM((micro, width), F32),
            dma((8, max(chunks, 4))),
            dma((4,)),
            dma((n,)),
            dma((n,)),
            dma((nblk,)),
            dma((nblk,)),
            dma((3, n)),
            dma((3, n)),
            dma((2, n)),
            dma((2, n)),
            dma((n,)),
            dma((n,)),
        ],
        compiler_params=pltpu.CompilerParams(
            collective_id=0, has_side_effects=True, vmem_limit_bytes=63 * 1024 * 1024
        ),
        cost_estimate=pl.CostEstimate(
            flops=rows * weight_bytes, bytes_accessed=weight_bytes, transcendentals=0
        ),
    )(*operands)


def local(n, *args):
    token_ids, embed_table = args[0], args[2]
    width, hidden_cols = embed_table.shape[1], args[7].shape[1]
    rows_here, micro = token_ids.shape
    kc = next((k for k in (1024, 512, 256, LANES) if width % k == 0), 0)
    fits = (
        rows_here == 1
        and n % 4 == 0
        and kc > 0
        and width % (n * HD) == 0
        and hidden_cols % LANES == 0
        and hidden_cols <= args[4].shape[1]
        and micro * (width // n // LANES) <= 8
        and (micro * n) % 16 == 0
        and embed_table.shape[0] <= LANES
        and sum(a.size * a.dtype.itemsize for a in args) <= 100 * 1024 * 1024
    )
    return local_fused(n, kc, *args) if fits else local_general(*args)


def solution(mesh):
    return jax.shard_map(
        functools.partial(local, mesh.shape["tensor"]),
        mesh=mesh,
        in_specs=(
            P("tensor", "groups"),
            P("groups"),
            P(),
            P(),
            P(None, "tensor"),
            P(None, "tensor"),
            P(),
            P(None, "tensor"),
            P(None, "tensor"),
            P("tensor", None),
            P(),
            P(None, "tensor"),
            P(None, "tensor"),
            P("tensor", None),
        ),
        out_specs=P("tensor", "groups", None),
        check_vma=False,
    )
```

time: 383 us -> 90.3 us (0.24)
  waiting for transfers between devices: 194 us -> 0 us
  blocking collectives: 100 us -> 0 us
  Pallas kernels: 0 us -> 88.7 us
  matrix products: 51.3 us -> 0 us
  between operations: 13.6 us -> 0.01 us
  other arithmetic: 8.77 us -> 0 us
  starting transfers between devices: 7.26 us -> 0 us
  local copies, waits for them, and re-layouts: 6.84 us -> 1.36 us
    all_gather x5 -> x0, blocking collectives: 100 us -> none  [the longest x3 61.8 us: spread_rows(): lax.all_gather(local_rows, 'tensor', axis=0, tiled=True)]
    unnamed x3 -> x0, waiting for transfers between devices: 90.6 us -> none
    psum x1 -> x0, waiting for transfers between devices: 90.3 us -> none  [local(): first_all = lax.psum(partial_all, 'tensor')]
    pallas_call x0 -> x1, Pallas kernels: none -> 88.7 us  [local_fused(): pl.pallas_call(functools.partial(fused_kernel, n, micro, vocab, kc), out_...]
    dot_general x9 -> x0, matrix products: 51.3 us -> none  [the longest x2 13.7 us: local_hidden(): jnp.einsum('pmd,dc->pmc', normed, gate_mat, preferred_element_type=jnp.fl...]
    all_to_all x2 -> x0, waiting for transfers between devices: 13.4 us -> none  [to_tokens(): lax.all_to_all(columns, 'tensor', split_axis=0, concat_axis=2, tiled=True)]
    all_to_all x2 -> x0, starting transfers between devices: 7 us -> none  [to_tokens(): lax.all_to_all(columns, 'tensor', split_axis=0, concat_axis=2, tiled=True)]
    convert_element_type x5 -> x0, other arithmetic: 3.87 us -> none  [the longest x1 2.02 us: local(): return after_second.astype(jnp.bfloat16)]
  transfers between devices with their start and end apart: 4 -> 0, of which waited for: 4 -> 0; matrix products, arithmetic and copies ran while one was open for 0% -> 0% of each run, Pallas kernels for 0% -> 0%
where the time goes in v1:
time: 90.3 us; the launch traced here: 90.1 us
  Pallas kernels  88.7 us (98%)
  local copies, waits for them, and re-layouts  1.36 us (2%)
    pallas_call x1, Pallas kernels, local_fused(): pl.pallas_call(functools.partial(fused_kernel, n, micro, vocab, kc), out_...  88.7 us

profile of v1, /device:TPU:0, one launch (start us, length us, event | category | flops | bytes accessed | tf_op | source)
XLA Modules:
  0.0 90.1 jit_solution(17965806728505513642)
XLA Ops:
  0.0 88.7 %shard_map.136 = bf16[1,2,6144]{2,1,0:T(2,128)(2,1)} custom-call(s32[1,2]{1,0:T(1,128)} %tok_ref.1, s32[2]{0:T(128)} %len_ref.1, bf16[64,6144]{1,0:T(8,128)(2,1)} %emb_hbm.1, f32[1,6144]{1,0:T(1,128)} %bitcast.3, bf16[6144,1152]{1,0:T(8,128)(2,1)} %wq_hbm.1, bf16[6144,384]{1,0:T(8,128)(2,1)} %wo_hbm.1, f32[1,6144]{1,0:T(1,128)} %bitcast.4, ...), custom_call_target="tpu_custom_call" | custom-call | flops 3047424512 | bytes 95232016 | tf_op jit(solution)/shard_map/pallas_call | solution.py:454
  88.7 1.4 %copy.16 = bf16[1,2,6144]{2,1,0:T(2,128)(2,1)} copy(bf16[1,2,6144]{2,1,0:T(2,128)(2,1)} %shard_map.136) | data formatting | bytes 49152

commit v2 on v1

--- a/solution.py
+++ b/solution.py
@@ -132,7 +132,8 @@
     def row_chunk(ref, c):
         return ref.at[pl.ds(c * kc, kc)]
 
-    dk = hidden_cols // 4
+    dparts = 8
+    dk = hidden_cols // dparts
 
     def w_copies(which):
         if which == "q":
@@ -156,12 +157,15 @@
         row = 6 if which == "d1" else 7
         return [
             pltpu.make_async_copy(src.at[pl.ds(c * dk, dk)], buf_d.at[pl.ds(c * dk, dk)], w_sem.at[row, c])
-            for c in range(4)
+            for c in range(dparts)
         ]
 
-    def start_all(which):
-        for cp in w_copies(which):
+    pending = []
+
+    def issue(count):
+        for cp in pending[:count]:
             cp.start()
+        del pending[:count]
 
     def wait_all(which):
         for cp in w_copies(which):
@@ -175,9 +179,8 @@
     ]
     for cp in small:
         cp.start()
-    start_all("q")
-    start_all("o")
-    start_all("g1")
+    pending.extend(w_copies("q") + w_copies("o") + w_copies("g1") + w_copies("u1") + w_copies("d1"))
+    issue(chunks // 2)
 
     tile_row = lax.broadcasted_iota(jnp.int32, (8, LANES), 0)
     tile = jnp.zeros((8, LANES), jnp.int32)
@@ -196,6 +199,7 @@
     ]
     for cp in tok_sends:
         cp.start()
+    issue(chunks - chunks // 2)
     for k in range(1, n):
         src = lax.rem(me + n - k, n)
         rcopy(toks.at[src], toks.at[src], small_send.at[k], small_recv.at[k], src).wait_recv()
@@ -254,9 +258,8 @@
         def _():
             pltpu.make_async_copy(blocks.at[j], qkv.at[slot], q_recv.at[slot]).start()
 
-    start_all("u1")
-    start_all("d1")
-    start_all("g2")
+    pending.extend(w_copies("g2"))
+    issue(chunks + 2 * chunks // 3)
 
     for slot in range(nblk):
         pltpu.make_async_copy(blocks.at[0], qkv.at[slot], q_recv.at[slot]).wait()
@@ -293,15 +296,18 @@
             send(me, k, zmove(me, k))
         send(me, xbase, xpeer)
         send(me, cbase, cpeer)
+        issue(1)
         for k in range(1, nz):
             src = zmove(me, -k)
             arrive(src, k)
             send(src, xbase + k, xpeer)
             send(src, cbase + k, cpeer)
+            issue(1)
         for k in range(nz):
             src = zmove(xpeer, -k)
             arrive(src, xbase + k)
             send(src, cbase + nz + k, cpeer)
+            issue(1)
         xc = cpeer + 2 - 4 * xbit
         for k in range(nz):
             arrive(zmove(cpeer, -k), cbase + k)
@@ -316,6 +322,7 @@
     o_copies = w_copies("o")
     for c in range(chunks):
         o_copies[c].wait()
+        issue(1)
         part += jnp.dot(
             normed[:, c * kc : (c + 1) * kc], buf_o[c * kc : (c + 1) * kc, :], preferred_element_type=F32
         )
@@ -358,6 +365,9 @@
             cp = rcopy(cout.at[ph, j], crecv.at[ph, j], rs_send.at[ph, j], rs_recv.at[ph, j], cpeer)
             cp.start()
             sends.append(cp)
+            issue(1)
+        if ph == 0:
+            pending.extend(w_copies("d2"))
         for k in range(nz):
             sends[k].wait_recv()
             xout[ph, k] = (acc[k] + crecv[ph, k].astype(F32)).astype(BF16)
@@ -367,6 +377,7 @@
             )
             cp.start()
             sends.append(cp)
+            issue(1)
         for k in list(range(1, nz)) + [0]:
             sends[nz + k].wait_recv()
             sends[2 * nz + k].wait_recv()
@@ -386,17 +397,18 @@
             own[...] = own[...] + zrecv[ph, k].astype(F32)
         return sends
 
+    issue(len(pending))
     hidden = feed(buf_g, buf_u, ("g1", "u1"), 1)
-    start_all("u2")
+    pending.extend(w_copies("u2"))
     wait_all("d1")
     sends2 = down_reduce(hidden, 0)
-    start_all("d2")
     full[2, me] = own[...].astype(BF16)
     sends3 = gather(2)
     for s in range(n):
         sl = slice(s * shard, (s + 1) * shard)
         resid[:, sl] = resid[:, sl] + full[2, s].astype(F32)
 
+    issue(len(pending))
     hidden = feed(buf_a, buf_g, ("g2", "u2"), 2)
     wait_all("d2")
     sends4 = down_reduce(hidden, 1)
@@ -482,7 +494,7 @@
             pltpu.VMEM((n, 8, LANES), F32),
             pltpu.VMEM((n, 8, LANES), F32),
             pltpu.VMEM((micro, width), F32),
-            dma((8, max(chunks, 4))),
+            dma((8, max(chunks, 8))),
             dma((4,)),
             dma((n,)),
             dma((n,)),

time: 90.3 us -> 87.8 us (0.972)
  Pallas kernels: 88.7 us -> 86.3 us
    pallas_call x1, Pallas kernels: 88.7 us -> 86.3 us  [local_fused(): pl.pallas_call(functools.partial(fused_kernel, n, micro, vocab, kc), out_...]
where the time goes in v2:
time: 87.8 us; the launch traced here: 87.6 us
  Pallas kernels  86.3 us (98%)
  local copies, waits for them, and re-layouts  1.36 us (2%)
    pallas_call x1, Pallas kernels, local_fused(): pl.pallas_call(functools.partial(fused_kernel, n, micro, vocab, kc), out_...  86.3 us

profile of v2, /device:TPU:0, one launch (start us, length us, event | category | flops | bytes accessed | tf_op | source)
XLA Modules:
  0.0 87.6 jit_solution(5118901009550062563)
XLA Ops:
  0.0 86.3 %shard_map.136 = bf16[1,2,6144]{2,1,0:T(2,128)(2,1)} custom-call(s32[1,2]{1,0:T(1,128)} %tok_ref.1, s32[2]{0:T(128)} %len_ref.1, bf16[64,6144]{1,0:T(8,128)(2,1)} %emb_hbm.1, f32[1,6144]{1,0:T(1,128)} %bitcast.3, bf16[6144,1152]{1,0:T(8,128)(2,1)} %wq_hbm.1, bf16[6144,384]{1,0:T(8,128)(2,1)} %wo_hbm.1, f32[1,6144]{1,0:T(1,128)} %bitcast.4, ...), custom_call_target="tpu_custom_call" | custom-call | flops 3047424512 | bytes 95232016 | tf_op jit(solution)/shard_map/pallas_call | solution.py:466
  86.3 1.4 %copy.16 = bf16[1,2,6144]{2,1,0:T(2,128)(2,1)} copy(bf16[1,2,6144]{2,1,0:T(2,128)(2,1)} %shard_map.136) | data formatting | bytes 49152

commit v3 on v2

--- a/solution.py
+++ b/solution.py
@@ -96,7 +96,7 @@
     buf_a, buf_o, buf_g, buf_u, buf_d,
     emb_ref, gain_ref,
     toks, onehot, resid, normed, blocks, qkv, full, acc, cout, crecv, xout, xrecv, zout, zrecv,
-    own, fin, finr, rows_out,
+    own, fin, finr, rows_out, oacc, gacc, uacc, stat,
     w_sem, e_sem, small_send, small_recv, q_send, q_recv, ag_send, ag_recv,
     rs_send, rs_recv, f_send, f_recv,
 ):
@@ -228,8 +228,9 @@
         for c in range(chunks):
             sl = slice(c * kc, (c + 1) * kc)
             normed[:, sl] = ((resid[:, sl] - mean) * inv * gain_ref[index, :, sl]).astype(BF16)
-
-    norm_into(0)
+        return mean
+
+    mean0 = norm_into(0)
 
     part = jnp.zeros((rows, nblk * HD), F32)
     q_copies = w_copies("q")
@@ -259,7 +260,7 @@
             pltpu.make_async_copy(blocks.at[j], qkv.at[slot], q_recv.at[slot]).start()
 
     pending.extend(w_copies("g2"))
-    issue(chunks + 2 * chunks // 3)
+    issue(3 * chunks)
 
     for slot in range(nblk):
         pltpu.make_async_copy(blocks.at[0], qkv.at[slot], q_recv.at[slot]).wait()
@@ -279,7 +280,7 @@
         numerator = jnp.dot(weights.astype(BF16), qkv[2 * hpd + h], preferred_element_type=F32)
         full[0, me, :, h * HD : (h + 1) * HD] = (numerator / denominator).astype(BF16)
 
-    def gather(ph):
+    def gather(ph, work):
         buf = full.at[ph]
         sends = []
 
@@ -297,119 +298,138 @@
         send(me, xbase, xpeer)
         send(me, cbase, cpeer)
         issue(1)
+        arrive(cpeer, cbase)
+        work(me // 2)
         for k in range(1, nz):
             src = zmove(me, -k)
             arrive(src, k)
             send(src, xbase + k, xpeer)
             send(src, cbase + k, cpeer)
             issue(1)
-        for k in range(nz):
+
+        def forward(k):
             src = zmove(xpeer, -k)
             arrive(src, xbase + k)
             send(src, cbase + nz + k, cpeer)
             issue(1)
+
         xc = cpeer + 2 - 4 * xbit
+        for k in range(1, nz):
+            arrive(zmove(cpeer, -k), cbase + k)
+            work(zmove(me, -k) // 2)
+            forward(k - 1)
+        forward(nz - 1)
         for k in range(nz):
-            arrive(zmove(cpeer, -k), cbase + k)
             arrive(zmove(xc, -k), cbase + nz + k)
+            work(zmove(xpeer, -k) // 2)
         return sends
 
-    sends0 = gather(0)
-    for s in range(n):
-        normed[:, s * shard : (s + 1) * shard] = full[0, s]
-
-    part = jnp.zeros((rows, shard), F32)
-    o_copies = w_copies("o")
-    for c in range(chunks):
-        o_copies[c].wait()
-        issue(1)
-        part += jnp.dot(
-            normed[:, c * kc : (c + 1) * kc], buf_o[c * kc : (c + 1) * kc, :], preferred_element_type=F32
-        )
-    full[1, me] = part.astype(BF16)
-    sends1 = gather(1)
-    for s in range(n):
-        sl = slice(s * shard, (s + 1) * shard)
-        resid[:, sl] = resid[:, sl] + full[1, s].astype(F32)
-
-    def feed(gate_buf, up_buf, names, index):
-        norm_into(index)
-        g_copies, u_copies = w_copies(names[0]), w_copies(names[1])
-        gated = jnp.zeros((rows, hidden_cols), F32)
-        lifted = jnp.zeros((rows, hidden_cols), F32)
-        for c in range(chunks):
-            x = normed[:, c * kc : (c + 1) * kc]
-            g_copies[c].wait()
-            gated += jnp.dot(x, gate_buf[c * kc : (c + 1) * kc, :hidden_cols], preferred_element_type=F32)
-        for c in range(chunks):
-            x = normed[:, c * kc : (c + 1) * kc]
-            u_copies[c].wait()
-            lifted += jnp.dot(x, up_buf[c * kc : (c + 1) * kc, :], preferred_element_type=F32)
-        return (gated / (1.0 + jnp.exp(-gated)) * lifted).astype(BF16)
+    def pair_of(ph, q):
+        return jnp.concatenate([full[ph, 2 * q], full[ph, 2 * q + 1]], axis=1)
+
+    def pair_span(q):
+        return pl.ds(pl.multiple_of(q * 2 * shard, LANES), 2 * shard)
+
+    wait_all("o")
+    oacc[...] = jnp.zeros_like(oacc)
+
+    def out_work(q):
+        oacc[...] += jnp.dot(pair_of(0, q), buf_o[pair_span(q), :], preferred_element_type=F32)
+
+    sends0 = gather(0, out_work)
+    full[1, me] = oacc[...].astype(BF16)
+    def feed(ph, gate_buf, up_buf, index, mean_before):
+        gacc[...] = jnp.zeros_like(gacc)
+        uacc[...] = jnp.zeros_like(uacc)
+        stat[...] = jnp.zeros_like(stat)
+
+        def work(q):
+            span = pair_span(q)
+            x = resid[:, span] + pair_of(ph, q).astype(F32)
+            resid[:, span] = x
+            cen = x - mean_before
+            stat[0] += jnp.sum(cen, axis=1, keepdims=True)
+            stat[1] += jnp.sum(cen * cen, axis=1, keepdims=True)
+            gain = gain_ref[index, :, span]
+            lhs = jnp.concatenate([cen * gain, jnp.broadcast_to(gain, (16, 2 * shard))], axis=0).astype(BF16)
+            gacc[...] += jnp.dot(lhs, gate_buf[span, :hidden_cols], preferred_element_type=F32)
+            uacc[...] += jnp.dot(lhs, up_buf[span, :], preferred_element_type=F32)
+
+        sends = gather(ph, work)
+        shift = stat[0] * (1.0 / width)
+        inv = lax.rsqrt(stat[1] * (1.0 / width) - shift * shift + 1e-05)
+        gated = inv * (gacc[:rows, :] - shift * gacc[rows : rows + 1, :])
+        lifted = inv * (uacc[:rows, :] - shift * uacc[rows : rows + 1, :])
+        hidden = (gated / (1.0 + jnp.exp(-gated)) * lifted).astype(BF16)
+        return hidden, mean_before + shift, sends
 
     def down_reduce(hidden, ph):
-        sends = []
-        for j in range(2 * nz):
+        sends = {}
+
+        def send(idx, src, dst, dev):
+            cp = rcopy(src, dst, rs_send.at[ph, idx], rs_recv.at[ph, idx], dev)
+            cp.start()
+            sends[idx] = cp
+
+        def column_sum(j):
             k = j % nz
             xsel = (1 - xbit) if j < nz else xbit
             q = lax.rem(zpos + k, nz) * 2 + xsel
-            both = jnp.dot(
-                hidden,
-                buf_d[:, pl.ds(pl.multiple_of(q * 2 * shard, LANES), 2 * shard)],
-                preferred_element_type=F32,
-            )
+            both = jnp.dot(hidden, buf_d[:, pair_span(q)], preferred_element_type=F32)
             left, right = both[:, :shard], both[:, shard:]
             is_left = jnp.zeros((rows, shard), jnp.int32) + core == 0
             acc[j] = jnp.where(is_left, left, right)
             cout[ph, j] = jnp.where(is_left, right, left).astype(BF16)
-            cp = rcopy(cout.at[ph, j], crecv.at[ph, j], rs_send.at[ph, j], rs_recv.at[ph, j], cpeer)
-            cp.start()
-            sends.append(cp)
-            issue(1)
-        if ph == 0:
-            pending.extend(w_copies("d2"))
-        for k in range(nz):
+            send(j, cout.at[ph, j], crecv.at[ph, j], cpeer)
+
+        def along_x(k):
             sends[k].wait_recv()
             xout[ph, k] = (acc[k] + crecv[ph, k].astype(F32)).astype(BF16)
-            cp = rcopy(
-                xout.at[ph, k], xrecv.at[ph, k],
-                rs_send.at[ph, 2 * nz + k], rs_recv.at[ph, 2 * nz + k], xpeer,
-            )
-            cp.start()
-            sends.append(cp)
-            issue(1)
-        for k in list(range(1, nz)) + [0]:
+            send(2 * nz + k, xout.at[ph, k], xrecv.at[ph, k], xpeer)
+
+        def along_z(k):
             sends[nz + k].wait_recv()
             sends[2 * nz + k].wait_recv()
             val = acc[nz + k] + crecv[ph, nz + k].astype(F32) + xrecv[ph, k].astype(F32)
             if k:
                 zout[ph, k] = val.astype(BF16)
-                cp = rcopy(
-                    zout.at[ph, k], zrecv.at[ph, k],
-                    rs_send.at[ph, 3 * nz + k], rs_recv.at[ph, 3 * nz + k], zmove(me, k),
-                )
-                cp.start()
-                sends.append(cp)
+                send(3 * nz + k, zout.at[ph, k], zrecv.at[ph, k], zmove(me, k))
             else:
                 own[...] = val
+
+        order = list(range(1, nz)) + [0]
+        for k in order:
+            column_sum(k)
+            issue(1)
+        for t, k in enumerate(order):
+            column_sum(nz + k)
+            issue(1)
+            along_x(k)
+            if t >= 2:
+                along_z(order[t - 2])
+        if ph == 0:
+            pending.extend(w_copies("d2"))
+        for k in order[max(nz - 2, 0) :]:
+            along_z(k)
         for k in range(1, nz):
-            sends[3 * nz + k - 1].wait_recv()
+            sends[3 * nz + k].wait_recv()
             own[...] = own[...] + zrecv[ph, k].astype(F32)
-        return sends
-
+        return list(sends.values())
+
+    wait_all("g1")
+    wait_all("u1")
+    hidden, mean1, sends1 = feed(1, buf_g, buf_u, 1, mean0)
     issue(len(pending))
-    hidden = feed(buf_g, buf_u, ("g1", "u1"), 1)
     pending.extend(w_copies("u2"))
+    issue(2)
     wait_all("d1")
     sends2 = down_reduce(hidden, 0)
+    issue(2)
     full[2, me] = own[...].astype(BF16)
-    sends3 = gather(2)
-    for s in range(n):
-        sl = slice(s * shard, (s + 1) * shard)
-        resid[:, sl] = resid[:, sl] + full[2, s].astype(F32)
-
+    wait_all("g2")
+    wait_all("u2")
+    hidden, _, sends3 = feed(2, buf_a, buf_g, 2, mean1)
     issue(len(pending))
-    hidden = feed(buf_a, buf_g, ("g2", "u2"), 2)
     wait_all("d2")
     sends4 = down_reduce(hidden, 1)
     own[...] = own[...] + resid[:, pl.ds(pl.multiple_of(me * shard, LANES), shard)]
@@ -494,6 +514,10 @@
             pltpu.VMEM((n, 8, LANES), F32),
             pltpu.VMEM((n, 8, LANES), F32),
             pltpu.VMEM((micro, width), F32),
+            pltpu.VMEM((rows, shard), F32),
+            pltpu.VMEM((rows + 16, hidden_cols), F32),
+            pltpu.VMEM((rows + 16, hidden_cols), F32),
+            pltpu.VMEM((2, rows, 1), F32),
             dma((8, max(chunks, 8))),
             dma((4,)),
             dma((n,)),

time: 87.8 us -> 76.7 us (0.87)
  Pallas kernels: 86.3 us -> 75.1 us
    pallas_call x1, Pallas kernels: 86.3 us -> 75.1 us  [local_fused(): pl.pallas_call(functools.partial(fused_kernel, n, micro, vocab, kc), out_...]
where the time goes in v3:
time: 76.7 us; the launch traced here: 76.5 us
  Pallas kernels  75.1 us (98%)
  local copies, waits for them, and re-layouts  1.36 us (2%)
    pallas_call x1, Pallas kernels, local_fused(): pl.pallas_call(functools.partial(fused_kernel, n, micro, vocab, kc), out_...  75.1 us

profile of v3, /device:TPU:0, one launch (start us, length us, event | category | flops | bytes accessed | tf_op | source)
XLA Modules:
  0.0 76.5 jit_solution(4399986463073232165)
XLA Ops:
  0.0 75.1 %shard_map.136 = bf16[1,2,6144]{2,1,0:T(2,128)(2,1)} custom-call(s32[1,2]{1,0:T(1,128)} %tok_ref.1, s32[2]{0:T(128)} %len_ref.1, bf16[64,6144]{1,0:T(8,128)(2,1)} %emb_hbm.1, f32[1,6144]{1,0:T(1,128)} %bitcast.3, bf16[6144,1152]{1,0:T(8,128)(2,1)} %wq_hbm.1, bf16[6144,384]{1,0:T(8,128)(2,1)} %wo_hbm.1, f32[1,6144]{1,0:T(1,128)} %bitcast.4, ...), custom_call_target="tpu_custom_call" | custom-call | flops 3047424512 | bytes 95232016 | tf_op jit(solution)/shard_map/pallas_call | solution.py:486
  75.1 1.4 %copy.16 = bf16[1,2,6144]{2,1,0:T(2,128)(2,1)} copy(bf16[1,2,6144]{2,1,0:T(2,128)(2,1)} %shard_map.136) | data formatting | bytes 49152
